TPU v7x, 32 devices: a whole 2x2x4 slice. The times are simulated.
32 devices in a mesh: groups: 2 (over y), ex: 4 (over z), layer: 2 (over x), rep: 2 (over core).
Axes of the slice: x: 2, y: 2, z: 4, core: 2. Of those that a mesh axis runs over, the one named last changes fastest.
Arguments:
- features: bfloat16 [8192, 4, 256], P(('groups', 'ex'), 'layer'), parts along dimension 0, may hold values from -6 to 6
- pair_list: int32 [3, 8, 4], P(None, ('groups', 'ex'), 'rep'), parts along dimension 1, may hold values from 0 to 3, as said below
- pair_count: int32 [8, 2], P(('groups', 'ex'), 'rep'), parts along dimension 0, may hold values from 1 to 2
Outputs:
- scores: float32 [8192], P(('groups', 'ex')), parts along dimension 0
There are 2 independent parts, one for each index of `groups`. A program takes and returns all parts, laid end to end along the dimension named above; each array names one. Nothing has to cross between parts.
Inputs may be any that keep to these rules, and one draw needn't show every extreme that they name: `pair_list`: row 0 names a block of the owner itself and row 2 a block of the owner named in row 1, both in 0 to 3; row 1 is in 0 to 3, and the 4 entries of row 1 of one owner are all different. Only the first pair_count entries of each index of rep are read.
All inputs are finite; a program needn't handle non-finite values.
Results may differ from a plain program's by a relative error of at most 0.004.
Values may be sent and summed in bfloat16 or wider, within the bound.
A program may use at most 64 MiB of HBM per device.

v0:
```python
import jax
import jax.numpy as jnp
from jax import lax
from jax.sharding import PartitionSpec as P

BLK = 256


def on_device(features, pair_list, pair_count):
    example_rows = features.shape[0]
    block_count = example_rows // BLK
    flat = features.reshape(example_rows, -1)
    width = flat.shape[1]
    squares = jnp.sum(jnp.square(flat.astype(jnp.float32)), axis=1)
    squares = lax.psum(squares, "layer")
    unit = (flat.astype(jnp.float32) * lax.rsqrt(squares + 1e-06)[:, None]).astype(jnp.bfloat16)
    unit_blocks = unit.reshape(block_count, BLK, width)
    mine_block = pair_list[0, 0]
    peer_owner = pair_list[1, 0]
    peer_block = pair_list[2, 0]
    live_count = pair_count[0, 0]
    slot_total = mine_block.shape[0]
    live = jnp.arange(slot_total, dtype=jnp.int32) < live_count
    owner_total = lax.axis_size("ex")
    matching = (peer_owner[None, :] == jnp.arange(owner_total, dtype=jnp.int32)[:, None]) & live[
        None, :
    ]
    requests = jnp.sum(jnp.where(matching, peer_block[None, :], 0), axis=1)[:, None]
    asked = lax.all_to_all(requests, "ex", split_axis=0, concat_axis=0, tiled=True)[:, 0]
    outgoing = jnp.take(unit_blocks, asked, axis=0)
    incoming = lax.all_to_all(outgoing, "ex", split_axis=0, concat_axis=0, tiled=True)
    group_total = lax.axis_size("layer")
    quarter = lax.axis_index("layer")
    same_block = (peer_owner == lax.axis_index("ex")) & (peer_block == mine_block)
    own_onehot = (mine_block[:, None] == jnp.arange(block_count, dtype=jnp.int32)[None, :]).astype(
        jnp.float32
    )
    matching_float = matching.astype(jnp.float32)
    local = slot_total // group_total
    partner_stack = jnp.take(incoming, peer_owner, axis=0)
    partner_full = lax.all_to_all(partner_stack, "layer", split_axis=0, concat_axis=2, tiled=True)
    own_full = lax.all_gather(unit_blocks, "layer", axis=2, tiled=True)
    first = quarter * local
    local_mine = lax.dynamic_slice_in_dim(mine_block, first, local)
    local_same = lax.dynamic_slice_in_dim(same_block, first, local)
    diagonal = jnp.arange(BLK)[:, None] == jnp.arange(BLK)[None, :]
    finished = jnp.clip(live_count - first, 0, local)

    def one_pair(slot, sums):
        row_store, column_store = sums
        left = lax.dynamic_index_in_dim(own_full, local_mine[slot], 0, keepdims=False)
        right = lax.dynamic_index_in_dim(partner_full, slot, 0, keepdims=False)
        left = left.reshape(BLK, group_total, width)
        right = right.reshape(BLK, group_total, width)
        partial_value = jnp.einsum(
            "igf,jgf->gij", left, right, preferred_element_type=jnp.float32
        ).astype(jnp.bfloat16)
        dots = jnp.sum(partial_value.astype(jnp.float32), axis=0)
        keep = jnp.logical_not(local_same[slot] & diagonal)
        kernel = jnp.where(keep, jnp.exp(20.0 * dots), 0.0)
        row_store = lax.dynamic_update_index_in_dim(row_store, jnp.sum(kernel, axis=1), slot, 0)
        column_store = lax.dynamic_update_index_in_dim(
            column_store, jnp.sum(kernel, axis=0), slot, 0
        )
        return (row_store, column_store)

    blank = jnp.zeros((local, BLK), jnp.float32)
    row_sums, column_sums = lax.fori_loop(0, finished, one_pair, (blank, blank))
    local_onehot = lax.dynamic_slice_in_dim(own_onehot, first, local, 0)
    row_full = jnp.einsum("sb,si->bi", local_onehot, row_sums, precision=lax.Precision.HIGHEST)
    local_matching = lax.dynamic_slice_in_dim(matching_float, first, local, 1)
    returned = jnp.dot(local_matching, column_sums, precision=lax.Precision.HIGHEST)
    back = lax.all_to_all(
        returned.astype(jnp.bfloat16), "ex", split_axis=0, concat_axis=0, tiled=True
    ).astype(returned.dtype)
    asked_onehot = (asked[:, None] == jnp.arange(block_count, dtype=jnp.int32)[None, :]).astype(
        jnp.float32
    )
    from_peers = jnp.einsum("wb,wj->bj", asked_onehot, back, precision=lax.Precision.HIGHEST)
    totals = lax.psum((row_full + from_peers).reshape(-1), ("layer", "rep"))
    return jnp.log1p(totals / BLK)


def solution(mesh):
    return jax.shard_map(
        on_device,
        mesh=mesh,
        in_specs=(
            P(("groups", "ex"), "layer", None),
            P(None, ("groups", "ex"), "rep"),
            P(("groups", "ex"), "rep"),
        ),
        out_specs=P(("groups", "ex")),
        check_vma=False,
    )
```

profile of v0, /device:TPU:0, one launch (start us, length us, event | category | flops | bytes accessed | tf_op | source)
XLA Modules:
  0.0 105.9 jit_solution(14541812109675714714)
XLA Ops:
  6.5 1.0 slice_reduce_fusion.2
  8.3 0.7 copy.15
  9.0 6.3 %all-to-all-start = ((s32[4,1,1]{2,1,0:T(1,128)}), s32[4,1,1]{2,1,0:T(1,128)S(1)}, u32[]{:S(2)}, u32[]{:S(2)}) async-start(s32[4,1,1]{2,1,0:T(1,128)} %copy.15), calls=%async_computation | async-start | bytes 4096 | tf_op jit(solution)/shard_map/all_to_all | solution.py:29
  15.3 1.6 %reshape.132 = f32[4,256,512]{2,1,0:T(8,128)S(1)} reshape(bf16[1024,2,256]{2,1,0:T(2,128)(2,1)} %param.5) | data formatting | bytes 3145728 | tf_op jit(solution)/shard_map/convert_element_type | solution.py:16
  17.0 2.5 %multiply_reduce_fusion = f32[1024]{0:T(1024)S(1)} fusion(bf16[1024,2,256]{2,1,0:T(2,128)(2,1)S(1)} %copy-done.1), kind=kLoop, calls=%fused_computation.3 | loop fusion | flops 1571840 | bytes 1052672 | tf_op jit(solution)/shard_map/reduce_sum | solution.py:14
  19.5 4.9 %psum.14 = f32[1024]{0:T(1024)S(1)} all-reduce(f32[1024]{0:T(1024)S(1)} %multiply_reduce_fusion), channel_id=1, replica_groups=mesh['groups'=2,'ex'=4,'layer'=2,'rep'=2] {'layer'}, use_global_device_ids=true, to_apply=%region_1.0 | all-reduce | flops 1024 | bytes 8192 | tf_op jit(solution)/shard_map/psum | solution.py:15
  24.9 0.6 gather_fusion
  25.5 1.1 %broadcast_select_fusion = bf16[4,256,512]{2,1,0:T(8,128)(2,1)} fusion(bf16[4,256,512]{2,1,0:T(8,128)(2,1)S(1)} %gather_fusion, pred[4]{0:T(512)(128)(4,1)S(1)} %compare_and_fusion), kind=kLoop, calls=%fused_computation.9 | loop fusion | flops 524288 | bytes 2097156 | tf_op jit(solution)/shard_map/jit(_take)/select_n | solution.py:30
  26.7 5.1 %all-to-all-start.1 = ((bf16[4,256,512]{2,1,0:T(8,128)(2,1)}), bf16[4,256,512]{2,1,0:T(8,128)(2,1)S(1)}, u32[]{:S(2)}, u32[]{:S(2)}) async-start(bf16[4,256,512]{2,1,0:T(8,128)(2,1)} %broadcast_select_fusion), calls=%async_computation.1 | async-start | bytes 2097152 | tf_op jit(solution)/shard_map/all_to_all | solution.py:31
  31.8 0.7 all-gather.2.cloned.1.call-update
  32.5 23.2 %all-to-all-done.1 = bf16[4,256,512]{2,1,0:T(8,128)(2,1)S(1)} async-done(((bf16[4,256,512]{2,1,0:T(8,128)(2,1)}), bf16[4,256,512]{2,1,0:T(8,128)(2,1)S(1)}, u32[]{:S(2)}, u32[]{:S(2)}) %all-to-all-start.1) | async-done | bytes 1048608 | tf_op jit(solution)/shard_map/all_to_all | solution.py:31
  55.8 0.6 gather_fusion.1
  56.4 0.9 broadcast_select_fusion.1
  57.3 3.5 %all-to-all-start.2 = ((bf16[2,256,512]{2,1,0:T(8,128)(2,1)}), bf16[2,256,512]{2,1,0:T(8,128)(2,1)S(1)}, u32[]{:S(2)}, u32[]{:S(2)}) async-start(bf16[2,256,512]{2,1,0:T(8,128)(2,1)} %broadcast_select_fusion.1), calls=%async_computation.2 | async-start | bytes 1048576 | tf_op jit(solution)/shard_map/all_to_all | solution.py:41
  60.8 0.5 constant_dynamic-slice_fusion.1
  62.7 0.7 dynamic_slice.23
  64.0 10.0 %all-gather.2.cloned.1.call-done = bf16[4,256,1024]{2,1,0:T(8,128)(2,1)} async-done(((bf16[4,256,512]{2,1,0:T(8,128)(2,1)}), bf16[4,256,1024]{2,1,0:T(8,128)(2,1)}) %all-gather.2.cloned.1.call-update) | async-done | bytes 2097168 | tf_op jit(solution)/shard_map/all_gather | solution.py:42
  74.0 1.1 %constant_dynamic-slice_fusion = bf16[1,256,1024]{2,1,0:T(8,128)(2,1)S(1)} fusion(bf16[4,256,1024]{2,1,0:T(8,128)(2,1)} %all-gather.2.cloned.1.call-done, s32[]{:T(128)S(6)} %select_n.72), kind=kLoop, calls=%fused_computation.40 | loop fusion | bytes 1048580 | tf_op jit(solution)/shard_map/while/body/jit(dynamic_index_in_dim)/dynamic_slice | solution.py:51
  75.7 0.8 fusion.5
  76.5 0.6 broadcast_in_dim.68
  77.1 0.6 broadcast_in_dim.68.clone
  77.7 1.2 %while.16 = (s32[]{:T(128)}, f32[1,256]{1,0:T(1,128)}, f32[1,256]{1,0:T(1,128)}, s32[]{:T(128)}, f32[256]{0:T(256)S(1)}, /*index=5*/f32[256]{0:T(256)S(1)}, s32[]{:T(128)}) while((s32[]{:T(128)}, f32[1,256]{1,0:T(1,128)}, f32[1,256]{1,0:T(1,128)}, s32[]{:T(128)}, f32[256]{0:T(256)S(1)}, /*index=5*/f32[256]{0:T(256)S(1)}, s32[]{:T(128)}) %tuple.38), condition=%wide.region_7.8_spmd, body=%wide.region_6.7_spmd.sunk | while | flops 2 | bytes 4173 | solution.py:68
  77.7 0.6 copy.33
  78.2 0.6 copy.34
  78.8 0.7 fusion.7
  80.1 0.7 reduce.10
  80.7 0.6 reshape.156
  81.3 5.0 %all-to-all-start.3 = ((bf16[4,2,128]{2,1,0:T(2,128)(2,1)}), bf16[4,2,128]{2,1,0:T(2,128)(2,1)S(1)}, u32[]{:S(2)}, u32[]{:S(2)}) async-start(bf16[4,2,128]{2,1,0:T(2,128)(2,1)} %reshape.156), calls=%async_computation.3 | async-start | bytes 4096 | tf_op jit(solution)/shard_map/all_to_all | solution.py:73
  86.3 5.5 %all-to-all-done.3 = bf16[4,2,128]{2,1,0:T(2,128)(2,1)S(1)} async-done(((bf16[4,2,128]{2,1,0:T(2,128)(2,1)}), bf16[4,2,128]{2,1,0:T(2,128)(2,1)S(1)}, u32[]{:S(2)}, u32[]{:S(2)}) %all-to-all-start.3) | async-done | bytes 2080 | tf_op jit(solution)/shard_map/all_to_all | solution.py:73
  91.8 0.9 fusion.2
  92.7 5.7 %psum.15 = f32[1024]{0:T(1024)S(1)} all-reduce(f32[1024]{0:T(1024)S(1)} %bitcast.46), channel_id=1, replica_groups=mesh['groups'=2,'ex'=4,'layer'=2,'rep'=2] {'layer','rep'}, use_global_device_ids=true, to_apply=%region_8.9 | all-reduce | flops 1024 | bytes 8192 | tf_op jit(solution)/shard_map/psum | solution.py:80
  98.4 0.6 multiply_log-plus-one_fusion
  (27 shorter events, 1.7 us)
Async XLA Ops:
  6.5 10.4 %copy-start.1 = (bf16[1024,2,256]{2,1,0:T(2,128)(2,1)S(1)}, bf16[1024,2,256]{2,1,0:T(2,128)(2,1)}, u32[]{:S(2)}) copy-start(bf16[1024,2,256]{2,1,0:T(2,128)(2,1)} %param.5) | copy-start | bytes 3145732
  9.0 15.7 %all-to-all-start = ((s32[4,1,1]{2,1,0:T(1,128)}), s32[4,1,1]{2,1,0:T(1,128)S(1)}, u32[]{:S(2)}, u32[]{:S(2)}) async-start(s32[4,1,1]{2,1,0:T(1,128)} %copy.15), calls=%async_computation | async-start | bytes 4096 | tf_op jit(solution)/shard_map/all_to_all | solution.py:29
  24.7 2.0 %copy-start = (bf16[4,256,512]{2,1,0:T(8,128)(2,1)}, bf16[4,256,512]{2,1,0:T(8,128)(2,1)S(1)}, u32[]{:S(2)}) copy-start(bf16[4,256,512]{2,1,0:T(8,128)(2,1)S(1)} %multiply_convert_fusion) | copy-start | bytes 3145732
  26.7 29.1 %all-to-all-start.1 = ((bf16[4,256,512]{2,1,0:T(8,128)(2,1)}), bf16[4,256,512]{2,1,0:T(8,128)(2,1)S(1)}, u32[]{:S(2)}, u32[]{:S(2)}) async-start(bf16[4,256,512]{2,1,0:T(8,128)(2,1)} %broadcast_select_fusion), calls=%async_computation.1 | async-start | bytes 2097152 | tf_op jit(solution)/shard_map/all_to_all | solution.py:31
  31.8 42.2 %all-gather.2.cloned.1.call-start = ((), (), s32[]{:S(2)}) async-start(), calls=%async_computation.4 | async-start | bytes 3145728 | tf_op jit(solution)/shard_map/all_gather | solution.py:42
  57.3 18.0 %all-to-all-start.2 = ((bf16[2,256,512]{2,1,0:T(8,128)(2,1)}), bf16[2,256,512]{2,1,0:T(8,128)(2,1)S(1)}, u32[]{:S(2)}, u32[]{:S(2)}) async-start(bf16[2,256,512]{2,1,0:T(8,128)(2,1)} %broadcast_select_fusion.1), calls=%async_computation.2 | async-start | bytes 1048576 | tf_op jit(solution)/shard_map/all_to_all | solution.py:41
  81.3 10.4 %all-to-all-start.3 = ((bf16[4,2,128]{2,1,0:T(2,128)(2,1)}), bf16[4,2,128]{2,1,0:T(2,128)(2,1)S(1)}, u32[]{:S(2)}, u32[]{:S(2)}) async-start(bf16[4,2,128]{2,1,0:T(2,128)(2,1)} %reshape.156), calls=%async_computation.3 | async-start | bytes 4096 | tf_op jit(solution)/shard_map/all_to_all | solution.py:73
Sparse Core Ops, SparseCore 0:
  34.1 39.8 all-gather.1
where the time goes:
time: 107 us; the launch traced here: 106 us
  waiting for transfers between devices  39.4 us (37%)
  starting transfers between devices  19.9 us (19%)
  between operations  16.2 us (15%)
  blocking collectives  10.7 us (10%)
  local copies, waits for them, and re-layouts  10.4 us (10%)
  other arithmetic  8.05 us (8%)
  matrix products  1.28 us (1%)
    all_to_all x1, waiting for transfers between devices, on_device(): lax.all_to_all(outgoing, 'ex', split_axis=0, concat_axis=0, tiled=True)  23.2 us
    all_gather x1, waiting for transfers between devices, on_device(): own_full = lax.all_gather(unit_blocks, 'layer', axis=2, tiled=True)  10 us
    all_to_all x1, starting transfers between devices, on_device(): lax.all_to_all(requests, 'ex', split_axis=0, concat_axis=0, tiled=True)  6.32 us
    psum x1, blocking collectives, on_device(): totals = lax.psum((row_full + from_peers).reshape(-1), ('layer', 'rep'))  5.74 us
    all_to_all x1, waiting for transfers between devices, on_device(): lax.all_to_all(returned.astype(jnp.bfloat16), 'ex', split_axis=0, concat_...  5.46 us
    all_to_all x1, starting transfers between devices, on_device(): lax.all_to_all(outgoing, 'ex', split_axis=0, concat_axis=0, tiled=True)  5.09 us
    all_to_all x1, starting transfers between devices, on_device(): lax.all_to_all(returned.astype(jnp.bfloat16), 'ex', split_axis=0, concat_...  4.97 us
    psum x1, blocking collectives, on_device(): squares = lax.psum(squares, 'layer')  4.95 us
  transfers between devices with their start and end apart: 5, of which 3 were waited for; matrix products, arithmetic and copies ran while one was open for 8% of the time, Pallas kernels for 0%

commit v1 on v0

v1 whole, which is shorter than its diff:
```python
import functools

import jax
import jax.numpy as jnp
from jax import lax
from jax.experimental import pallas as pl
from jax.experimental.pallas import tpu as pltpu
from jax.sharding import PartitionSpec as P

BLK = 256
MESH = pl.DeviceIdType.MESH
CONTRACT_LAST = (((1,), (1,)), ((), ()))


def body(N, L, R, feat, plist, pcount, out, tab, stage, arow, csend, crecv, sq, isend, irecv, xsend, xrecv,
         rsend, rrecv, ctab, tab_s, tab_r, a_s, a_r, c_s, c_r, q_s, q_r, i_s, i_r, x_s, x_r, r_s, r_r, t_s, t_r):
    NB = feat.shape[0]
    slots = plist.shape[2]
    J = N // R
    HB = BLK // L
    e, l, r = lax.axis_index("ex"), lax.axis_index("layer"), lax.axis_index("rep")

    def place(d, dl, dr):
        return {"ex": lax.rem(e + d, N), "layer": lax.rem(l + dl, L), "rep": lax.rem(r + dr, R)}

    def remote(src, dst, ss, rs, target):
        return pltpu.make_async_remote_copy(
            src_ref=src, dst_ref=dst, send_sem=ss, recv_sem=rs, device_id=target, device_id_type=MESH
        )

    barrier = pltpu.get_barrier_semaphore()

    def greet(i, carry):
        pl.semaphore_signal(
            barrier, inc=1, device_id=place(i // (L * R), lax.rem(i // R, L), lax.rem(i, R)), device_id_type=MESH
        )
        return carry

    lax.fori_loop(1, N * L * R, greet, 0)

    rows_iota = lax.broadcasted_iota(jnp.int32, tab.shape[1:], 0)
    table = jnp.zeros(tab.shape[1:], jnp.int32)
    count = pcount[0, 0]
    for s in range(slots):
        code = jnp.where(s < count, 1 + plist[0, 0, s] + 256 * plist[2, 0, s], 0)
        table = table + jnp.where(rows_iota == plist[1, 0, s], code, 0)
    tab[r] = table

    pl.semaphore_wait(barrier, N * L * R - 1)

    tab_copies = []
    for dr in range(1, R):
        copy = remote(tab.at[r], tab.at[r], tab_s.at[dr - 1], tab_r.at[dr - 1], place(0, 0, dr))
        copy.start()
        tab_copies.append(copy)

    ones = jnp.ones((8, feat.shape[2]), jnp.bfloat16)
    for b in range(NB):
        x = feat[b].astype(jnp.float32)
        x2 = x * x
        high = x2.astype(jnp.bfloat16)
        low = (x2 - high.astype(jnp.float32)).astype(jnp.bfloat16)
        s2 = lax.dot_general(ones, high, CONTRACT_LAST, preferred_element_type=jnp.float32)
        s2 = s2 + lax.dot_general(ones, low, CONTRACT_LAST, preferred_element_type=jnp.float32)
        sq[l, b : b + 1, :] = s2[0:1, :]

    q_copies = []
    for dl in range(1, L):
        copy = remote(sq.at[l], sq.at[l], q_s.at[dl - 1], q_r.at[dl - 1], place(0, dl, 0))
        copy.start()
        q_copies.append(copy)

    for copy in tab_copies:
        copy.wait()
    table = tab[0]
    for i in range(1, R):
        table = table + tab[i]

    codes, a_copies, c_copies = [], [], []
    for j in range(J):
        d = R * j + r
        p = lax.rem(e + d, N)
        code = jnp.max(jnp.where(rows_iota == p, table, 0))
        codes.append(code)
        mine = jnp.maximum(code - 1, 0) & 255
        stage[j] = feat[mine]
        csend[j] = jnp.full(csend.shape[1:], code, jnp.int32)
        target = {"ex": p}
        a_copy = remote(stage.at[j], arow.at[j], a_s.at[j], a_r.at[j], target)
        c_copy = remote(csend.at[j], crecv.at[j], c_s.at[j], c_r.at[j], target)
        if j == 0:

            @pl.when(r == 0)
            def _():
                arow[0] = stage[0]
                crecv[0] = csend[0]

            @pl.when(r != 0)
            def _():
                a_copy.start()
                c_copy.start()

        else:
            a_copy.start()
            c_copy.start()
        a_copies.append(a_copy)
        c_copies.append(c_copy)

    for copy in q_copies:
        copy.wait()
    total_sq = sq[0]
    for i in range(1, L):
        total_sq = total_sq + sq[i]
    inv = lax.rsqrt(total_sq + 1e-06)

    i_copies = []
    for j in range(J):
        mine = jnp.maximum(codes[j] - 1, 0) & 255
        pick = jnp.zeros((1, BLK), jnp.float32)
        for b in range(NB):
            pick = jnp.where(mine == b, inv[b : b + 1, :], pick)
        isend[j] = pick
        copy = remote(isend.at[j], irecv.at[j], i_s.at[j], i_r.at[j], {"ex": lax.rem(e + R * j + r, N)})
        if j == 0:

            @pl.when(r == 0)
            def _():
                irecv[0] = isend[0]

            @pl.when(r != 0)
            def _():
                copy.start()

        else:
            copy.start()
        i_copies.append(copy)

    at_row = lax.broadcasted_iota(jnp.int32, (HB, BLK), 0) + l * HB
    at_column = lax.broadcasted_iota(jnp.int32, (HB, BLK), 1)
    spot = at_row == at_column
    columns = [jnp.zeros((1, BLK), jnp.float32) for _ in range(NB)]
    x_copies, own, rights = [], [], []
    for j in range(J):
        if j == 0:

            @pl.when(r != 0)
            def _():
                c_copies[0].wait()
                a_copies[0].wait()
                i_copies[0].wait()

        else:
            c_copies[j].wait()
            a_copies[j].wait()
            i_copies[j].wait()
        code = jnp.max(crecv[j])
        peer = jnp.maximum(code - 1, 0) // 256
        right = feat[peer]
        rights.append((code, peer))
        for dl in range(1, L):
            other = lax.rem(l + dl, L)
            left = arow[j, pl.ds(pl.multiple_of(other * HB, HB), HB), :]
            part = lax.dot_general(left, right, CONTRACT_LAST, preferred_element_type=jnp.float32)
            xsend[j, dl - 1] = part.astype(jnp.bfloat16)
            copy = remote(
                xsend.at[j, dl - 1], xrecv.at[j, dl - 1], x_s.at[j, dl - 1], x_r.at[j, dl - 1], place(0, dl, 0)
            )
            copy.start()
            x_copies.append(copy)
        left = arow[j, pl.ds(pl.multiple_of(l * HB, HB), HB), :]
        own.append(lax.dot_general(left, right, CONTRACT_LAST, preferred_element_type=jnp.float32))

    r_copies = []
    for j in range(J):
        dots = own[j]
        for dl in range(1, L):
            x_copies[j * (L - 1) + dl - 1].wait()
            dots = dots + xrecv[j, dl - 1].astype(jnp.float32)
        code, peer = rights[j]
        inv_row = jnp.sum(jnp.where(spot, irecv[j], 0.0), axis=1, keepdims=True)
        inv_column = jnp.zeros((1, BLK), jnp.float32)
        for b in range(NB):
            inv_column = jnp.where(peer == b, inv[b : b + 1, :], inv_column)
        kern = jnp.exp(20.0 * (dots * inv_row * inv_column))
        if j == 0:
            same = (r == 0) & ((jnp.maximum(code - 1, 0) & 255) == peer)
            kern = jnp.where(spot, kern * jnp.where(same, 0.0, 1.0), kern)
        row_sums = jnp.sum(kern, axis=1, keepdims=True)
        rsend[j] = jnp.sum(jnp.where(spot, row_sums, 0.0), axis=0, keepdims=True)
        column_sums = jnp.sum(kern, axis=0, keepdims=True)
        for b in range(NB):
            columns[b] = columns[b] + jnp.where((peer == b) & (code > 0), column_sums, 0.0)
        slot = e * L + l
        back = N - (R * j + r)
        for dl in range(L):
            for dr in range(R):
                k = dl * R + dr
                copy = remote(rsend.at[j], rrecv.at[slot], r_s.at[j, k], r_r.at[slot], place(back, dl, dr))
                if j == 0 and k == 0:

                    @pl.when(r == 0)
                    def _():
                        rrecv[slot] = rsend[0]

                    @pl.when(r != 0)
                    def _():
                        copy.start()

                else:
                    copy.start()
                r_copies.append(copy)

    mine_slot = l * R + r
    for b in range(NB):
        ctab[mine_slot, b : b + 1, :] = columns[b]
    t_copies = []
    for k in range(1, L * R):
        copy = remote(
            ctab.at[mine_slot], ctab.at[mine_slot], t_s.at[k - 1], t_r.at[k - 1], place(0, k // R, k % R)
        )
        copy.start()
        t_copies.append(copy)

    for k in range(1, L * R):
        t_copies[k - 1].wait()
    for d in range(N):
        p = lax.rem(e + d, N)
        for dl in range(L):
            slot = p * L + lax.rem(l + dl, L)
            copy = remote(rsend.at[0], rrecv.at[slot], r_s.at[0, 0], r_r.at[slot], place(0, 0, 1))
            if d == 0 and dl == 0:

                @pl.when(r != 0)
                def _():
                    copy.wait_recv()

            else:
                copy.wait_recv()

    totals = ctab[0]
    for i in range(1, L * R):
        totals = totals + ctab[i]
    block_iota = lax.broadcasted_iota(jnp.int32, (NB, BLK), 0)
    for p in range(N):
        got = rrecv[p * L]
        for i in range(1, L):
            got = got + rrecv[p * L + i]
        code = table[p : p + 1, :]
        code = jnp.concatenate([code] * (BLK // 128), axis=1)
        live = (code > 0) & ((jnp.maximum(code - 1, 0) & 255) == block_iota)
        totals = totals + jnp.where(live, got, 0.0)
    for b in range(NB):
        for h in range(BLK // 128):
            out[b * (BLK // 128) + h : b * (BLK // 128) + h + 1, :] = totals[b : b + 1, h * 128 : (h + 1) * 128]

    for n, copy in enumerate(r_copies):
        if n == 0:

            @pl.when(r != 0)
            def _():
                r_copies[0].wait_send()

        else:
            copy.wait_send()


def on_device(sizes, features, pair_list, pair_count):
    N, L, R = sizes
    rows = features.shape[0]
    blocks = features.reshape(rows // BLK, BLK, -1)
    NB, _, width = blocks.shape
    J = N // R
    HB = BLK // L
    table_rows = -(-N // 8) * 8
    dma = pltpu.SemaphoreType.DMA
    vmem = pl.BlockSpec(memory_space=pltpu.VMEM)
    smem = pl.BlockSpec(memory_space=pltpu.SMEM)
    totals = pl.pallas_call(
        functools.partial(body, N, L, R),
        out_shape=jax.ShapeDtypeStruct((rows // 128, 128), jnp.float32),
        in_specs=[vmem, smem, smem],
        out_specs=vmem,
        scratch_shapes=[
            pltpu.VMEM((R, table_rows, 128), jnp.int32),
            pltpu.VMEM((J, BLK, width), jnp.bfloat16),
            pltpu.VMEM((J, BLK, width), jnp.bfloat16),
            pltpu.VMEM((J, 8, 128), jnp.int32),
            pltpu.VMEM((J, 8, 128), jnp.int32),
            pltpu.VMEM((L, NB, BLK), jnp.float32),
            pltpu.VMEM((J, 1, BLK), jnp.float32),
            pltpu.VMEM((J, 1, BLK), jnp.float32),
            pltpu.VMEM((J, L - 1, HB, BLK), jnp.bfloat16),
            pltpu.VMEM((J, L - 1, HB, BLK), jnp.bfloat16),
            pltpu.VMEM((J, 1, BLK), jnp.float32),
            pltpu.VMEM((N * L, 1, BLK), jnp.float32),
            pltpu.VMEM((L * R, NB, BLK), jnp.float32),
            dma((R - 1,)), dma((R - 1,)),
            dma((J,)), dma((J,)),
            dma((J,)), dma((J,)),
            dma((L - 1,)), dma((L - 1,)),
            dma((J,)), dma((J,)),
            dma((J, L - 1)), dma((J, L - 1)),
            dma((J, L * R)), dma((N * L,)),
            dma((L * R - 1,)), dma((L * R - 1,)),
        ],
        compiler_params=pltpu.CompilerParams(
            collective_id=0, has_side_effects=True, vmem_limit_bytes=48 * 1024 * 1024
        ),
    )(blocks, pair_list, pair_count)
    return jnp.log1p(totals / BLK).reshape(-1)


def solution(mesh):
    sizes = (mesh.shape["ex"], mesh.shape["layer"], mesh.shape["rep"])
    return jax.shard_map(
        functools.partial(on_device, sizes),
        mesh=mesh,
        in_specs=(
            P(("groups", "ex"), "layer", None),
            P(None, ("groups", "ex"), "rep"),
            P(("groups", "ex"), "rep"),
        ),
        out_specs=P(("groups", "ex")),
        check_vma=False,
    )
```

time: 107 us -> 31.4 us (0.29)
  waiting for transfers between devices: 39.4 us -> 0 us
  Pallas kernels: 0 us -> 28.1 us
  starting transfers between devices: 19.9 us -> 0 us
  between operations: 16.2 us -> 0.68 us
  blocking collectives: 10.7 us -> 0 us
  local copies, waits for them, and re-layouts: 10.4 us -> 1.84 us
  other arithmetic: 8.05 us -> 0.6 us
  matrix products: 1.28 us -> 0 us
    all_to_all x4 -> x0, waiting for transfers between devices: 28.7 us -> none  [the longest x1 23.2 us: on_device(): lax.all_to_all(outgoing, 'ex', split_axis=0, concat_axis=0, tiled=True)]
    pallas_call x0 -> x1, Pallas kernels: none -> 28.1 us  [on_device(): pl.pallas_call(functools.partial(body, N, L, R), out_shape=jax.ShapeDtype...]
    all_to_all x4 -> x0, starting transfers between devices: 19.9 us -> none  [the longest x1 6.32 us: on_device(): lax.all_to_all(requests, 'ex', split_axis=0, concat_axis=0, tiled=True)]
    psum x2 -> x0, blocking collectives: 10.7 us -> none  [the longest x1 5.74 us: on_device(): totals = lax.psum((row_full + from_peers).reshape(-1), ('layer', 'rep'))]
    all_gather x1 -> x0, waiting for transfers between devices: 10 us -> none  [on_device(): own_full = lax.all_gather(unit_blocks, 'layer', axis=2, tiled=True)]
    reduce_sum x3 -> x0, other arithmetic: 3.47 us -> none  [the longest x1 2.55 us: on_device(): squares = jnp.sum(jnp.square(flat.astype(jnp.float32)), axis=1)]
    dynamic_slice x4 -> x0, local copies, waits for them, and re-layouts: 2.47 us -> none  [the longest x2 1.28 us: one_pair(): lax.dynamic_index_in_dim(own_full, local_mine[slot], 0, keepdims=False)]
    select_n x4 -> x0, other arithmetic: 2.06 us -> none  [the longest x2 1.15 us: on_device(): outgoing = jnp.take(unit_blocks, asked, axis=0)]
  transfers between devices with their start and end apart: 5 -> 0, of which waited for: 3 -> 0; matrix products, arithmetic and copies ran while one was open for 8% -> 0% of each run, Pallas kernels for 0% -> 0%
where the time goes in v1:
time: 31.4 us; the launch traced here: 31.3 us
  Pallas kernels  28.1 us (89%)
  local copies, waits for them, and re-layouts  1.84 us (6%)
  between operations  0.68 us (2%)
  other arithmetic  0.6 us (2%)
    pallas_call x1, Pallas kernels, on_device(): pl.pallas_call(functools.partial(body, N, L, R), out_shape=jax.ShapeDtype...  28.1 us
    reshape x1, local copies, waits for them, and re-layouts, on_device(): blocks = features.reshape(rows // BLK, BLK, -1)  1.73 us

profile of v1, /device:TPU:0, one launch (start us, length us, event | category | flops | bytes accessed | tf_op | source)
XLA Modules:
  0.0 31.3 jit_solution(13300549539267345940)
XLA Ops:
  0.0 0.0 copy-start
  0.7 0.0 copy-done
  0.7 0.1 copy.4.plist
  0.8 1.7 %reshape.6.feat = bf16[4,256,512]{2,1,0:T(8,128)(2,1)S(1)} reshape(bf16[1024,2,256]{2,1,0:T(2,128)(2,1)} %param.3) | data formatting | bytes 2097152 | tf_op jit(solution)/shard_map/reshape | solution.py:270
  2.5 28.1 %shard_map.37 = f32[8,128]{1,0:T(8,128)S(1)} custom-call(bf16[4,256,512]{2,1,0:T(8,128)(2,1)S(1)} %reshape.6.feat, s32[3,1,2]{2,1,0:T(1,128)S(1)} %copy.4.plist, s32[1,1]{1,0:T(1,128)S(6)} %copy.5.pcount), custom_call_target="tpu_custom_call" | custom-call | tf_op jit(solution)/shard_map/pallas_call | solution.py:278
  30.7 0.6 %log-plus-one_bitcast_fusion = f32[1024]{0:T(1024)} fusion(f32[8,128]{1,0:T(8,128)S(1)} %shard_map.37), kind=kLoop, calls=%fused_computation | loop fusion | flops 1024 | bytes 8192 | tf_op jit(solution)/shard_map/reshape | solution.py:310
Async XLA Ops:
  0.0 0.7 %copy-start = (s32[3,1,2]{0,2,1:T(2,128)S(1)}, s32[3,1,2]{0,2,1:T(2,128)}, u32[]{:S(2)}) copy-start(s32[3,1,2]{0,2,1:T(2,128)} %param.4) | copy-start | bytes 76

commit v2 on v1

--- a/solution.py
+++ b/solution.py
@@ -15,7 +15,7 @@
 def body(N, L, R, feat, plist, pcount, out, tab, stage, arow, csend, crecv, sq, isend, irecv, xsend, xrecv,
          rsend, rrecv, ctab, tab_s, tab_r, a_s, a_r, c_s, c_r, q_s, q_r, i_s, i_r, x_s, x_r, r_s, r_r, t_s, t_r):
     NB = feat.shape[0]
-    slots = plist.shape[2]
+    slots = plist.shape[1]
     J = N // R
     HB = BLK // L
     e, l, r = lax.axis_index("ex"), lax.axis_index("layer"), lax.axis_index("rep")
@@ -42,17 +42,9 @@
     table = jnp.zeros(tab.shape[1:], jnp.int32)
     count = pcount[0, 0]
     for s in range(slots):
-        code = jnp.where(s < count, 1 + plist[0, 0, s] + 256 * plist[2, 0, s], 0)
-        table = table + jnp.where(rows_iota == plist[1, 0, s], code, 0)
+        code = jnp.where(s < count, 1 + plist[0, s, 0] + 256 * plist[0, s, 2], 0)
+        table = table + jnp.where(rows_iota == plist[0, s, 1], code, 0)
     tab[r] = table
-
-    pl.semaphore_wait(barrier, N * L * R - 1)
-
-    tab_copies = []
-    for dr in range(1, R):
-        copy = remote(tab.at[r], tab.at[r], tab_s.at[dr - 1], tab_r.at[dr - 1], place(0, 0, dr))
-        copy.start()
-        tab_copies.append(copy)
 
     ones = jnp.ones((8, feat.shape[2]), jnp.bfloat16)
     for b in range(NB):
@@ -64,6 +56,14 @@
         s2 = s2 + lax.dot_general(ones, low, CONTRACT_LAST, preferred_element_type=jnp.float32)
         sq[l, b : b + 1, :] = s2[0:1, :]
 
+    pl.semaphore_wait(barrier, N * L * R - 1)
+
+    tab_copies = []
+    for dr in range(1, R):
+        copy = remote(tab.at[r], tab.at[r], tab_s.at[dr - 1], tab_r.at[dr - 1], place(0, 0, dr))
+        copy.start()
+        tab_copies.append(copy)
+
     q_copies = []
     for dl in range(1, L):
         copy = remote(sq.at[l], sq.at[l], q_s.at[dl - 1], q_r.at[dl - 1], place(0, dl, 0))
@@ -76,18 +76,26 @@
     for i in range(1, R):
         table = table + tab[i]
 
-    codes, a_copies, c_copies = [], [], []
-    for j in range(J):
-        d = R * j + r
-        p = lax.rem(e + d, N)
+    def part_rows(dl):
+        return pl.ds(pl.multiple_of(lax.rem(l + dl, L) * HB, HB), HB)
+
+    order = list(range(1, L)) + [0]
+    codes, c_copies = [], []
+    a_copies = {}
+    for j in range(J):
+        p = lax.rem(e + R * j + r, N)
         code = jnp.max(jnp.where(rows_iota == p, table, 0))
         codes.append(code)
         mine = jnp.maximum(code - 1, 0) & 255
         stage[j] = feat[mine]
         csend[j] = jnp.full(csend.shape[1:], code, jnp.int32)
         target = {"ex": p}
-        a_copy = remote(stage.at[j], arow.at[j], a_s.at[j], a_r.at[j], target)
         c_copy = remote(csend.at[j], crecv.at[j], c_s.at[j], c_r.at[j], target)
+        c_copies.append(c_copy)
+        for dl in order:
+            a_copies[j, dl] = remote(
+                stage.at[j, part_rows(dl)], arow.at[j, part_rows(dl)], a_s.at[j, dl], a_r.at[j, dl], target
+            )
         if j == 0:
 
             @pl.when(r == 0)
@@ -97,14 +105,23 @@
 
             @pl.when(r != 0)
             def _():
-                a_copy.start()
                 c_copy.start()
+                for dl in order[:-1]:
+                    a_copies[0, dl].start()
 
         else:
-            a_copy.start()
             c_copy.start()
-        a_copies.append(a_copy)
-        c_copies.append(c_copy)
+            for dl in order[:-1]:
+                a_copies[j, dl].start()
+    for j in range(J):
+        if j == 0:
+
+            @pl.when(r != 0)
+            def _():
+                a_copies[0, 0].start()
+
+        else:
+            a_copies[j, 0].start()
 
     for copy in q_copies:
         copy.wait()
@@ -139,42 +156,45 @@
     at_column = lax.broadcasted_iota(jnp.int32, (HB, BLK), 1)
     spot = at_row == at_column
     columns = [jnp.zeros((1, BLK), jnp.float32) for _ in range(NB)]
-    x_copies, own, rights = [], [], []
-    for j in range(J):
+    x_copies, rights = {}, []
+
+    def arrived(j, *copies):
         if j == 0:
 
             @pl.when(r != 0)
             def _():
-                c_copies[0].wait()
-                a_copies[0].wait()
-                i_copies[0].wait()
+                for copy in copies:
+                    copy.wait_recv()
 
         else:
-            c_copies[j].wait()
-            a_copies[j].wait()
-            i_copies[j].wait()
+            for copy in copies:
+                copy.wait_recv()
+
+    for j in range(J):
+        arrived(j, c_copies[j])
         code = jnp.max(crecv[j])
         peer = jnp.maximum(code - 1, 0) // 256
-        right = feat[peer]
         rights.append((code, peer))
         for dl in range(1, L):
-            other = lax.rem(l + dl, L)
-            left = arow[j, pl.ds(pl.multiple_of(other * HB, HB), HB), :]
-            part = lax.dot_general(left, right, CONTRACT_LAST, preferred_element_type=jnp.float32)
+            arrived(j, a_copies[j, dl])
+            part = lax.dot_general(
+                arow[j, part_rows(dl), :], feat[peer], CONTRACT_LAST, preferred_element_type=jnp.float32
+            )
             xsend[j, dl - 1] = part.astype(jnp.bfloat16)
             copy = remote(
                 xsend.at[j, dl - 1], xrecv.at[j, dl - 1], x_s.at[j, dl - 1], x_r.at[j, dl - 1], place(0, dl, 0)
             )
             copy.start()
-            x_copies.append(copy)
-        left = arow[j, pl.ds(pl.multiple_of(l * HB, HB), HB), :]
-        own.append(lax.dot_general(left, right, CONTRACT_LAST, preferred_element_type=jnp.float32))
+            x_copies[j, dl] = copy
 
     r_copies = []
     for j in range(J):
-        dots = own[j]
+        arrived(j, a_copies[j, 0], i_copies[j])
+        dots = lax.dot_general(
+            arow[j, part_rows(0), :], feat[rights[j][1]], CONTRACT_LAST, preferred_element_type=jnp.float32
+        )
         for dl in range(1, L):
-            x_copies[j * (L - 1) + dl - 1].wait()
+            x_copies[j, dl].wait_recv()
             dots = dots + xrecv[j, dl - 1].astype(jnp.float32)
         code, peer = rights[j]
         inv_row = jnp.sum(jnp.where(spot, irecv[j], 0.0), axis=1, keepdims=True)
@@ -253,14 +273,15 @@
         for h in range(BLK // 128):
             out[b * (BLK // 128) + h : b * (BLK // 128) + h + 1, :] = totals[b : b + 1, h * 128 : (h + 1) * 128]
 
-    for n, copy in enumerate(r_copies):
-        if n == 0:
-
-            @pl.when(r != 0)
-            def _():
-                r_copies[0].wait_send()
-
-        else:
+    for copy in r_copies[1:] + list(x_copies.values()):
+        copy.wait_send()
+    for j in range(1, J):
+        for copy in [c_copies[j], i_copies[j]] + [a_copies[j, dl] for dl in order]:
+            copy.wait_send()
+
+    @pl.when(r != 0)
+    def _():
+        for copy in [r_copies[0], c_copies[0], i_copies[0]] + [a_copies[0, dl] for dl in order]:
             copy.wait_send()
 
 
@@ -295,7 +316,7 @@
             pltpu.VMEM((N * L, 1, BLK), jnp.float32),
             pltpu.VMEM((L * R, NB, BLK), jnp.float32),
             dma((R - 1,)), dma((R - 1,)),
-            dma((J,)), dma((J,)),
+            dma((J, L)), dma((J, L)),
             dma((J,)), dma((J,)),
             dma((L - 1,)), dma((L - 1,)),
             dma((J,)), dma((J,)),
@@ -306,7 +327,7 @@
         compiler_params=pltpu.CompilerParams(
             collective_id=0, has_side_effects=True, vmem_limit_bytes=48 * 1024 * 1024
         ),
-    )(blocks, pair_list, pair_count)
+    )(blocks, pair_list.transpose(1, 2, 0), pair_count)
     return jnp.log1p(totals / BLK).reshape(-1)
 
 

time: 31.4 us -> 28.3 us (0.901)
  Pallas kernels: 28.1 us -> 25.1 us
    pallas_call x1, Pallas kernels: 28.1 us -> 25.1 us  [on_device(): pl.pallas_call(functools.partial(body, N, L, R), out_shape=jax.ShapeDtype...]
where the time goes in v2:
time: 28.3 us; the launch traced here: 28.2 us
  Pallas kernels  25.1 us (89%)
  local copies, waits for them, and re-layouts  1.75 us (6%)
  between operations  0.68 us (2%)
  other arithmetic  0.6 us (2%)
    pallas_call x1, Pallas kernels, on_device(): pl.pallas_call(functools.partial(body, N, L, R), out_shape=jax.ShapeDtype...  25.1 us
    reshape x1, local copies, waits for them, and re-layouts, on_device(): blocks = features.reshape(rows // BLK, BLK, -1)  1.74 us
    reshape x1, other arithmetic, on_device(): return jnp.log1p(totals / BLK).reshape(-1)  0.6 us

profile of v2, /device:TPU:0, one launch (start us, length us, event | category | flops | bytes accessed | tf_op | source)
XLA Modules:
  0.0 28.2 jit_solution(562890429954954286)
XLA Ops:
  0.7 0.0 copy-start
  0.7 1.7 %reshape.6.feat = bf16[4,256,512]{2,1,0:T(8,128)(2,1)S(1)} reshape(bf16[1024,2,256]{2,1,0:T(2,128)(2,1)} %param.3) | data formatting | bytes 2097152 | tf_op jit(solution)/shard_map/reshape | solution.py:291
  2.4 0.0 copy-done
  2.4 25.1 %shard_map.37 = f32[8,128]{1,0:T(8,128)S(1)} custom-call(bf16[4,256,512]{2,1,0:T(8,128)(2,1)S(1)} %reshape.6.feat, s32[1,2,3]{2,1,0:T(2,128)S(1)} %bitcast.3, s32[1,1]{1,0:T(1,128)S(6)} %copy.4.pcount), custom_call_target="tpu_custom_call" | custom-call | tf_op jit(solution)/shard_map/pallas_call | solution.py:299
  27.6 0.6 %log-plus-one_bitcast_fusion = f32[1024]{0:T(1024)} fusion(f32[8,128]{1,0:T(8,128)S(1)} %shard_map.37), kind=kLoop, calls=%fused_computation | loop fusion | flops 1024 | bytes 8192 | tf_op jit(solution)/shard_map/reshape | solution.py:331
Async XLA Ops:
  0.7 1.8 %copy-start = (s32[3,1,2]{0,2,1:T(2,128)S(1)}, s32[3,1,2]{0,2,1:T(2,128)}, u32[]{:S(2)}) copy-start(s32[3,1,2]{0,2,1:T(2,128)} %param.4) | copy-start | bytes 76

commit v3 on v2

--- a/solution.py
+++ b/solution.py
@@ -30,13 +30,21 @@
 
     barrier = pltpu.get_barrier_semaphore()
 
-    def greet(i, carry):
-        pl.semaphore_signal(
-            barrier, inc=1, device_id=place(i // (L * R), lax.rem(i // R, L), lax.rem(i, R)), device_id_type=MESH
-        )
-        return carry
-
-    lax.fori_loop(1, N * L * R, greet, 0)
+    def greet(d, dl, dr):
+        pl.semaphore_signal(barrier, inc=1, device_id=place(d, dl, dr), device_id_type=MESH)
+
+    for j in reversed(range(J)):
+        d = R * j + r
+        if j == 0:
+
+            @pl.when(r != 0)
+            def _():
+                greet(r, 0, 0)
+
+        else:
+            greet(d, 0, 0)
+    for k in range(1, L * R):
+        greet(0, k // R, k % R)
 
     rows_iota = lax.broadcasted_iota(jnp.int32, tab.shape[1:], 0)
     table = jnp.zeros(tab.shape[1:], jnp.int32)
@@ -56,7 +64,8 @@
         s2 = s2 + lax.dot_general(ones, low, CONTRACT_LAST, preferred_element_type=jnp.float32)
         sq[l, b : b + 1, :] = s2[0:1, :]
 
-    pl.semaphore_wait(barrier, N * L * R - 1)
+    pl.semaphore_wait(barrier, J - 1 + jnp.minimum(r, 1) + L * R - 1)
+
 
     tab_copies = []
     for dr in range(1, R):

time: 28.3 us -> 27.8 us (0.982)
  Pallas kernels: 25.1 us -> 24.6 us
    pallas_call x1, Pallas kernels: 25.1 us -> 24.6 us  [on_device(): pl.pallas_call(functools.partial(body, N, L, R), out_shape=jax.ShapeDtype...]
where the time goes in v3:
time: 27.8 us; the launch traced here: 27.6 us
  Pallas kernels  24.6 us (88%)
  local copies, waits for them, and re-layouts  1.75 us (6%)
  between operations  0.68 us (2%)
  other arithmetic  0.6 us (2%)
    pallas_call x1, Pallas kernels, on_device(): pl.pallas_call(functools.partial(body, N, L, R), out_shape=jax.ShapeDtype...  24.6 us
    reshape x1, local copies, waits for them, and re-layouts, on_device(): blocks = features.reshape(rows // BLK, BLK, -1)  1.74 us
    reshape x1, other arithmetic, on_device(): return jnp.log1p(totals / BLK).reshape(-1)  0.6 us

profile of v3, /device:TPU:0, one launch (start us, length us, event | category | flops | bytes accessed | tf_op | source)
XLA Modules:
  0.0 27.6 jit_solution(8989876747324947070)
XLA Ops:
  0.7 0.0 copy-start
  0.7 1.7 %reshape.6.feat = bf16[4,256,512]{2,1,0:T(8,128)(2,1)S(1)} reshape(bf16[1024,2,256]{2,1,0:T(2,128)(2,1)} %param.3) | data formatting | bytes 2097152 | tf_op jit(solution)/shard_map/reshape | solution.py:300
  2.4 0.0 copy-done
  2.4 24.6 %shard_map.37 = f32[8,128]{1,0:T(8,128)S(1)} custom-call(bf16[4,256,512]{2,1,0:T(8,128)(2,1)S(1)} %reshape.6.feat, s32[1,2,3]{2,1,0:T(2,128)S(1)} %bitcast.3, s32[1,1]{1,0:T(1,128)S(6)} %copy.4.pcount), custom_call_target="tpu_custom_call" | custom-call | tf_op jit(solution)/shard_map/pallas_call | solution.py:308
  27.0 0.6 %log-plus-one_bitcast_fusion = f32[1024]{0:T(1024)} fusion(f32[8,128]{1,0:T(8,128)S(1)} %shard_map.37), kind=kLoop, calls=%fused_computation | loop fusion | flops 1024 | bytes 8192 | tf_op jit(solution)/shard_map/reshape | solution.py:340
Async XLA Ops:
  0.7 1.8 %copy-start = (s32[3,1,2]{0,2,1:T(2,128)S(1)}, s32[3,1,2]{0,2,1:T(2,128)}, u32[]{:S(2)}) copy-start(s32[3,1,2]{0,2,1:T(2,128)} %param.4) | copy-start | bytes 76

commit v4 on v3

--- a/solution.py
+++ b/solution.py
@@ -13,7 +13,7 @@
 
 
 def body(N, L, R, feat, plist, pcount, out, tab, stage, arow, csend, crecv, sq, isend, irecv, xsend, xrecv,
-         rsend, rrecv, ctab, tab_s, tab_r, a_s, a_r, c_s, c_r, q_s, q_r, i_s, i_r, x_s, x_r, r_s, r_r, t_s, t_r):
+         rsend, rrecv, ctab, scale, tab_s, tab_r, a_s, a_r, c_s, c_r, q_s, q_r, i_s, i_r, x_s, x_r, r_s, r_r, t_s, t_r):
     NB = feat.shape[0]
     slots = plist.shape[1]
     J = N // R
@@ -122,7 +122,7 @@
             c_copy.start()
             for dl in order[:-1]:
                 a_copies[j, dl].start()
-    for j in range(J):
+    for j in reversed(range(J)):
         if j == 0:
 
             @pl.when(r != 0)
@@ -165,6 +165,11 @@
     at_column = lax.broadcasted_iota(jnp.int32, (HB, BLK), 1)
     spot = at_row == at_column
     columns = [jnp.zeros((1, BLK), jnp.float32) for _ in range(NB)]
+    block_iota = lax.broadcasted_iota(jnp.int32, (NB, BLK), 0)
+    held = []
+    for p in range(N):
+        code = jnp.concatenate([table[p : p + 1, :]] * (BLK // 128), axis=1)
+        held.append((code > 0) & ((jnp.maximum(code - 1, 0) & 255) == block_iota))
     x_copies, rights = {}, []
 
     def arrived(j, *copies):
@@ -196,9 +201,17 @@
             copy.start()
             x_copies[j, dl] = copy
 
+    for j in range(J):
+        arrived(j, i_copies[j])
+        inv_row = jnp.sum(jnp.where(spot, irecv[j], 0.0), axis=1, keepdims=True)
+        inv_column = jnp.zeros((1, BLK), jnp.float32)
+        for b in range(NB):
+            inv_column = jnp.where(rights[j][1] == b, inv[b : b + 1, :], inv_column)
+        scale[j] = 20.0 * (inv_row * inv_column)
+
     r_copies = []
     for j in range(J):
-        arrived(j, a_copies[j, 0], i_copies[j])
+        arrived(j, a_copies[j, 0])
         dots = lax.dot_general(
             arow[j, part_rows(0), :], feat[rights[j][1]], CONTRACT_LAST, preferred_element_type=jnp.float32
         )
@@ -206,11 +219,7 @@
             x_copies[j, dl].wait_recv()
             dots = dots + xrecv[j, dl - 1].astype(jnp.float32)
         code, peer = rights[j]
-        inv_row = jnp.sum(jnp.where(spot, irecv[j], 0.0), axis=1, keepdims=True)
-        inv_column = jnp.zeros((1, BLK), jnp.float32)
-        for b in range(NB):
-            inv_column = jnp.where(peer == b, inv[b : b + 1, :], inv_column)
-        kern = jnp.exp(20.0 * (dots * inv_row * inv_column))
+        kern = jnp.exp(dots * scale[j])
         if j == 0:
             same = (r == 0) & ((jnp.maximum(code - 1, 0) & 255) == peer)
             kern = jnp.where(spot, kern * jnp.where(same, 0.0, 1.0), kern)
@@ -269,15 +278,11 @@
     totals = ctab[0]
     for i in range(1, L * R):
         totals = totals + ctab[i]
-    block_iota = lax.broadcasted_iota(jnp.int32, (NB, BLK), 0)
     for p in range(N):
         got = rrecv[p * L]
         for i in range(1, L):
             got = got + rrecv[p * L + i]
-        code = table[p : p + 1, :]
-        code = jnp.concatenate([code] * (BLK // 128), axis=1)
-        live = (code > 0) & ((jnp.maximum(code - 1, 0) & 255) == block_iota)
-        totals = totals + jnp.where(live, got, 0.0)
+        totals = totals + jnp.where(held[p], got, 0.0)
     for b in range(NB):
         for h in range(BLK // 128):
             out[b * (BLK // 128) + h : b * (BLK // 128) + h + 1, :] = totals[b : b + 1, h * 128 : (h + 1) * 128]
@@ -324,6 +329,7 @@
             pltpu.VMEM((J, 1, BLK), jnp.float32),
             pltpu.VMEM((N * L, 1, BLK), jnp.float32),
             pltpu.VMEM((L * R, NB, BLK), jnp.float32),
+            pltpu.VMEM((J, HB, BLK), jnp.float32),
             dma((R - 1,)), dma((R - 1,)),
             dma((J, L)), dma((J, L)),
             dma((J,)), dma((J,)),

time: 27.8 us -> 27.4 us (0.986); the launches traced: 27.6 us -> 26.9 us
  Pallas kernels: 24.6 us -> 23.8 us
    pallas_call x1, Pallas kernels: 24.6 us -> 23.8 us  [on_device(): pl.pallas_call(functools.partial(body, N, L, R), out_shape=jax.ShapeDtype...]
where the time goes in v4:
time: 27.4 us; the launch traced here: 26.9 us
  Pallas kernels  23.8 us (87%)
  local copies, waits for them, and re-layouts  1.75 us (6%)
  between operations  0.68 us (2%)
  other arithmetic  0.6 us (2%)
    pallas_call x1, Pallas kernels, on_device(): pl.pallas_call(functools.partial(body, N, L, R), out_shape=jax.ShapeDtype...  23.8 us
    reshape x1, local copies, waits for them, and re-layouts, on_device(): blocks = features.reshape(rows // BLK, BLK, -1)  1.74 us
    reshape x1, other arithmetic, on_device(): return jnp.log1p(totals / BLK).reshape(-1)  0.6 us

profile of v4, /device:TPU:0, one launch (start us, length us, event | category | flops | bytes accessed | tf_op | source)
XLA Modules:
  0.0 26.9 jit_solution(5060108762008172734)
XLA Ops:
  0.7 0.0 copy-start
  0.7 1.7 %reshape.6.feat = bf16[4,256,512]{2,1,0:T(8,128)(2,1)S(1)} reshape(bf16[1024,2,256]{2,1,0:T(2,128)(2,1)} %param.3) | data formatting | bytes 2097152 | tf_op jit(solution)/shard_map/reshape | solution.py:305
  2.4 0.0 copy-done
  2.4 23.8 %shard_map.37 = f32[8,128]{1,0:T(8,128)S(1)} custom-call(bf16[4,256,512]{2,1,0:T(8,128)(2,1)S(1)} %reshape.6.feat, s32[1,2,3]{2,1,0:T(2,128)S(1)} %bitcast.3, s32[1,1]{1,0:T(1,128)S(6)} %copy.4.pcount), custom_call_target="tpu_custom_call" | custom-call | tf_op jit(solution)/shard_map/pallas_call | solution.py:313
  26.3 0.6 %log-plus-one_bitcast_fusion = f32[1024]{0:T(1024)} fusion(f32[8,128]{1,0:T(8,128)S(1)} %shard_map.37), kind=kLoop, calls=%fused_computation | loop fusion | flops 1024 | bytes 8192 | tf_op jit(solution)/shard_map/reshape | solution.py:346
Async XLA Ops:
  0.7 1.8 %copy-start = (s32[3,1,2]{0,2,1:T(2,128)S(1)}, s32[3,1,2]{0,2,1:T(2,128)}, u32[]{:S(2)}) copy-start(s32[3,1,2]{0,2,1:T(2,128)} %param.4) | copy-start | bytes 76

commit v5 on v4

--- a/solution.py
+++ b/solution.py
@@ -89,18 +89,17 @@
         return pl.ds(pl.multiple_of(lax.rem(l + dl, L) * HB, HB), HB)
 
     order = list(range(1, L)) + [0]
-    codes, c_copies = [], []
-    a_copies = {}
-    for j in range(J):
+    codes, c_copies, a_copies = {}, {}, {}
+    for j in reversed(range(J)):
         p = lax.rem(e + R * j + r, N)
         code = jnp.max(jnp.where(rows_iota == p, table, 0))
-        codes.append(code)
+        codes[j] = code
         mine = jnp.maximum(code - 1, 0) & 255
         stage[j] = feat[mine]
         csend[j] = jnp.full(csend.shape[1:], code, jnp.int32)
         target = {"ex": p}
         c_copy = remote(csend.at[j], crecv.at[j], c_s.at[j], c_r.at[j], target)
-        c_copies.append(c_copy)
+        c_copies[j] = c_copy
         for dl in order:
             a_copies[j, dl] = remote(
                 stage.at[j, part_rows(dl)], arow.at[j, part_rows(dl)], a_s.at[j, dl], a_r.at[j, dl], target

time: 27.4 us -> 27.2 us (level)
  the two profiles are of different devices: /device:TPU:0 before, /device:TPU:9 now
where the time goes in v5:
time: 27.2 us; the launch traced here: 27 us
  Pallas kernels  24 us (88%)
  local copies, waits for them, and re-layouts  1.75 us (6%)
  between operations  0.68 us (2%)
  other arithmetic  0.6 us (2%)
    pallas_call x1, Pallas kernels, on_device(): pl.pallas_call(functools.partial(body, N, L, R), out_shape=jax.ShapeDtype...  24 us
    reshape x1, local copies, waits for them, and re-layouts, on_device(): blocks = features.reshape(rows // BLK, BLK, -1)  1.74 us
    reshape x1, other arithmetic, on_device(): return jnp.log1p(totals / BLK).reshape(-1)  0.6 us

profile of v5, /device:TPU:9, one launch (start us, length us, event | category | flops | bytes accessed | tf_op | source)
XLA Modules:
  0.0 27.0 jit_solution(16639550825100869797)
XLA Ops:
  0.7 0.0 copy-start
  0.7 1.7 %reshape.6.feat = bf16[4,256,512]{2,1,0:T(8,128)(2,1)S(1)} reshape(bf16[1024,2,256]{2,1,0:T(2,128)(2,1)} %param.3) | data formatting | bytes 2097152 | tf_op jit(solution)/shard_map/reshape | solution.py:304
  2.4 0.0 copy-done
  2.4 24.0 %shard_map.37 = f32[8,128]{1,0:T(8,128)S(1)} custom-call(bf16[4,256,512]{2,1,0:T(8,128)(2,1)S(1)} %reshape.6.feat, s32[1,2,3]{2,1,0:T(2,128)S(1)} %bitcast.3, s32[1,1]{1,0:T(1,128)S(6)} %copy.4.pcount), custom_call_target="tpu_custom_call" | custom-call | tf_op jit(solution)/shard_map/pallas_call | solution.py:312
  26.4 0.6 %log-plus-one_bitcast_fusion = f32[1024]{0:T(1024)} fusion(f32[8,128]{1,0:T(8,128)S(1)} %shard_map.37), kind=kLoop, calls=%fused_computation | loop fusion | flops 1024 | bytes 8192 | tf_op jit(solution)/shard_map/reshape | solution.py:345
Async XLA Ops:
  0.7 1.8 %copy-start = (s32[3,1,2]{0,2,1:T(2,128)S(1)}, s32[3,1,2]{0,2,1:T(2,128)}, u32[]{:S(2)}) copy-start(s32[3,1,2]{0,2,1:T(2,128)} %param.4) | copy-start | bytes 76

commit v6 on v5

--- a/solution.py
+++ b/solution.py
@@ -95,7 +95,8 @@
         code = jnp.max(jnp.where(rows_iota == p, table, 0))
         codes[j] = code
         mine = jnp.maximum(code - 1, 0) & 255
-        stage[j] = feat[mine]
+        for dl in order[:-1]:
+            stage[j, part_rows(dl), :] = feat[mine, part_rows(dl), :]
         csend[j] = jnp.full(csend.shape[1:], code, jnp.int32)
         target = {"ex": p}
         c_copy = remote(csend.at[j], crecv.at[j], c_s.at[j], c_r.at[j], target)
@@ -108,7 +109,7 @@
 
             @pl.when(r == 0)
             def _():
-                arow[0] = stage[0]
+                arow[0] = feat[mine]
                 crecv[0] = csend[0]
 
             @pl.when(r != 0)
@@ -122,6 +123,8 @@
             for dl in order[:-1]:
                 a_copies[j, dl].start()
     for j in reversed(range(J)):
+        mine = jnp.maximum(codes[j] - 1, 0) & 255
+        stage[j, part_rows(0), :] = feat[mine, part_rows(0), :]
         if j == 0:
 
             @pl.when(r != 0)

time: 27.2 us -> 27.2 us (level)
  the two profiles are of different devices: /device:TPU:9 before, /device:TPU:0 now
where the time goes in v6:
time: 27.2 us; the launch traced here: 26.7 us
  Pallas kernels  23.6 us (87%)
  local copies, waits for them, and re-layouts  1.75 us (6%)
  between operations  0.68 us (2%)
  other arithmetic  0.6 us (2%)
    pallas_call x1, Pallas kernels, on_device(): pl.pallas_call(functools.partial(body, N, L, R), out_shape=jax.ShapeDtype...  23.6 us
    reshape x1, local copies, waits for them, and re-layouts, on_device(): blocks = features.reshape(rows // BLK, BLK, -1)  1.74 us
    reshape x1, other arithmetic, on_device(): return jnp.log1p(totals / BLK).reshape(-1)  0.6 us

profile of v6, /device:TPU:0, one launch (start us, length us, event | category | flops | bytes accessed | tf_op | source)
XLA Modules:
  0.0 26.7 jit_solution(3248052277807363154)
XLA Ops:
  0.7 0.0 copy-start
  0.7 1.7 %reshape.6.feat = bf16[4,256,512]{2,1,0:T(8,128)(2,1)S(1)} reshape(bf16[1024,2,256]{2,1,0:T(2,128)(2,1)} %param.3) | data formatting | bytes 2097152 | tf_op jit(solution)/shard_map/reshape | solution.py:307
  2.4 0.0 copy-done
  2.4 23.6 %shard_map.37 = f32[8,128]{1,0:T(8,128)S(1)} custom-call(bf16[4,256,512]{2,1,0:T(8,128)(2,1)S(1)} %reshape.6.feat, s32[1,2,3]{2,1,0:T(2,128)S(1)} %bitcast.3, s32[1,1]{1,0:T(1,128)S(6)} %copy.4.pcount), custom_call_target="tpu_custom_call" | custom-call | tf_op jit(solution)/shard_map/pallas_call | solution.py:315
  26.0 0.6 %log-plus-one_bitcast_fusion = f32[1024]{0:T(1024)} fusion(f32[8,128]{1,0:T(8,128)S(1)} %shard_map.37), kind=kLoop, calls=%fused_computation | loop fusion | flops 1024 | bytes 8192 | tf_op jit(solution)/shard_map/reshape | solution.py:348
Async XLA Ops:
  0.7 1.8 %copy-start = (s32[3,1,2]{0,2,1:T(2,128)S(1)}, s32[3,1,2]{0,2,1:T(2,128)}, u32[]{:S(2)}) copy-start(s32[3,1,2]{0,2,1:T(2,128)} %param.4) | copy-start | bytes 76
